TPU v7x, 256 devices: a whole 4x4x8 slice. The times are simulated.
256 devices in a mesh: row: 16 (over z, core), col: 16 (over x, y).
Axes of the slice: x: 4, y: 4, z: 8, core: 2. Of those that a mesh axis runs over, the one named last changes fastest.
Arguments:
- activations: bfloat16 [512, 12288], P('col', 'row'), may hold values from -6 to 6
- output_grad: bfloat16 [512, 12288], P('col', 'row'), may hold values from -3 to 3
- up_weight: bfloat16 [12288, 24576], P('row', 'col'), may hold values from -0.0546875 to 0.0546875
- down_weight: bfloat16 [12288, 24576], P('row', 'col'), may hold values from -0.0390625 to 0.0390625
- up_bias: bfloat16 [24576], P('col'), may hold values from -4 to 4
Outputs:
- input_grad: bfloat16 [512, 12288], P('col', 'row')
- up_grad: bfloat16 [12288, 24576], P('row', 'col')
- down_grad: bfloat16 [12288, 24576], P('row', 'col')
- bias_grad: float32 [24576], P('col')
All inputs are finite; a program needn't handle non-finite values.
Results may differ from a plain program's by a relative error of at most 0.0049.
Values may be sent and summed in bfloat16 or wider, within the bound.
A program may use at most 64 MiB of HBM per device.

v0:
```python
import jax
import jax.numpy as jnp
from jax import lax
from jax.sharding import PartitionSpec as P


def gelu_parts(pre_act):
    coeff = 0.7978845608028654
    cubic = 0.044715
    inner = coeff * (pre_act + cubic * pre_act * pre_act * pre_act)
    tanh_val = jnp.tanh(inner)
    value = 0.5 * pre_act * (1.0 + tanh_val)
    slope = 0.5 * (1.0 + tanh_val) + 0.5 * pre_act * (1.0 - tanh_val * tanh_val) * coeff * (
        1.0 + 3.0 * cubic * pre_act * pre_act
    )
    return (value, slope)


def finish(stacked, up_bias, hidden_width):
    pre_act = stacked[:, :hidden_width] + up_bias.astype(jnp.float32)[None, :]
    hidden_grad = stacked[:, hidden_width:]
    value, slope = gelu_parts(pre_act)
    return ((hidden_grad * slope).astype(jnp.bfloat16), value.astype(jnp.bfloat16))


def body(activations, output_grad, up_weight, down_weight, up_bias):
    seen_acts, seen_grads = (
        lax.all_gather(activations, "col", axis=0, tiled=True),
        lax.all_gather(output_grad, "col", axis=0, tiled=True),
    )
    hidden_width = up_weight.shape[1]
    first = jnp.dot(seen_acts, up_weight, preferred_element_type=jnp.float32)
    second = jnp.dot(seen_grads, down_weight, preferred_element_type=jnp.float32)
    stacked = lax.psum_scatter(
        jnp.concatenate([first, second], axis=1), "row", scatter_dimension=0, tiled=True
    )
    act_grad, hidden_out = finish(stacked, up_bias, hidden_width)
    full_grad, full_hidden = (
        lax.all_gather(act_grad, "row", axis=0, tiled=True),
        lax.all_gather(hidden_out, "row", axis=0, tiled=True),
    )
    up_grad = lax.dot_general(
        seen_acts, full_grad, (((0,), (0,)), ((), ())), preferred_element_type=jnp.float32
    )
    down_grad = lax.dot_general(
        seen_grads, full_hidden, (((0,), (0,)), ((), ())), preferred_element_type=jnp.float32
    )
    bias_grad = jnp.sum(full_grad.astype(jnp.float32), axis=0)
    input_grad = lax.psum_scatter(
        lax.dot_general(
            full_grad, up_weight, (((1,), (1,)), ((), ())), preferred_element_type=jnp.float32
        ),
        "col",
        scatter_dimension=0,
        tiled=True,
    )
    return (
        input_grad.astype(jnp.bfloat16),
        up_grad.astype(jnp.bfloat16),
        down_grad.astype(jnp.bfloat16),
        bias_grad,
    )


def solution(mesh):
    placed = (P("col", "row"), P("col", "row"), P("row", "col"), P("row", "col"), P("col"))
    return jax.shard_map(
        body,
        mesh=mesh,
        in_specs=placed,
        out_specs=(P("col", "row"), P("row", "col"), P("row", "col"), P("col")),
        check_vma=False,
    )
```

profile of v0, /device:TPU:1, one launch (start us, length us, event | category | flops | bytes accessed | tf_op | source)
XLA Modules:
  0.0 298.8 jit_solution(11636415995311530946)
XLA Ops:
  7.2 0.0 reduce-scatter.3.cloned.1.call-start
  7.2 20.4 %all_gather.13 = bf16[512,768]{1,0:T(8,128)(2,1)S(1)} all-gather(bf16[32,768]{1,0:T(8,128)(2,1)} %param.6), channel_id=1, replica_groups=mesh['row'=16,'col'=16] {'col'}, dimensions={0}, use_global_device_ids=true | all-gather | bytes 835584 | tf_op jit(solution)/shard_map/all_gather | solution.py:29
  27.7 18.3 %all_gather.12 = bf16[512,768]{1,0:T(8,128)(2,1)S(1)} all-gather(bf16[32,768]{1,0:T(8,128)(2,1)} %param.5), channel_id=1, replica_groups=mesh['row'=16,'col'=16] {'col'}, dimensions={0}, use_global_device_ids=true | all-gather | bytes 835584 | tf_op jit(solution)/shard_map/all_gather | solution.py:28
  46.0 3.3 %fusion.10 = f32[512,1536]{1,0:T(8,128)S(1)} fusion(bf16[512,768]{1,0:T(8,128)(2,1)S(1)} %all_gather.13, bf16[768,1536]{1,0:T(8,128)(2,1)} %param.8), kind=kOutput, calls=%fused_computation.18 | convolution fusion | flops 1207959552 | bytes 6291456 | tf_op jit(solution)/shard_map/dot_general | solution.py:33
  49.3 1.4 fusion.9
  50.7 3.2 %pad_maximum_fusion = f32[512,3072]{1,0:T(8,128)} fusion(f32[512,1536]{1,0:T(8,128)S(1)} %fusion.10, f32[512,1536]{1,0:T(8,128)S(1)} %fusion.9), kind=kLoop, calls=%fused_computation | loop fusion | flops 1572864 | bytes 12582912 | tf_op jit(solution)/shard_map/concatenate | solution.py:35
  53.9 0.0 reduce-scatter.3.cloned.1.call-update
  54.0 0.0 all-gather.3.cloned.1.call-start
  54.0 0.6 copy-done.2
  54.6 73.8 %reduce-scatter.3.cloned.1.call-done = f32[32,3072]{1,0:T(8,128)} async-done(((f32[512,3072]{1,0:T(8,128)}), f32[32,3072]{1,0:T(8,128)}) %reduce-scatter.3.cloned.1.call-update) | async-done | bytes 393232 | tf_op jit(solution)/shard_map/reduce_scatter | solution.py:34
  128.4 1.8 multiply_convert_fusion
  130.3 0.0 all-gather.5.cloned.1.call-start
  130.3 0.7 all-gather.5.cloned.1.call-update
  131.0 0.0 reduce-scatter.5.cloned.1.call-start
  131.1 41.2 %all-gather.3.cloned.1.call-done = bf16[512,1536]{1,0:T(8,128)(2,1)} async-done(((bf16[32,1536]{1,0:T(8,128)(2,1)}), bf16[512,1536]{1,0:T(8,128)(2,1)}) %all-gather.3.cloned.1.call-update) | async-done | bytes 1572880 | tf_op jit(solution)/shard_map/all_gather | solution.py:39
  172.3 4.0 %fusion.11 = f32[512,768]{1,0:T(8,128)} fusion(bf16[512,1536]{1,0:T(8,128)(2,1)} %all-gather.3.cloned.1.call-done, bf16[768,1536]{1,0:T(8,128)(2,1)S(1)} %copy-done), kind=kOutput, calls=%fused_computation.19 | convolution fusion | flops 1207959552 | bytes 5505024 | tf_op jit(solution)/shard_map/dot_general | solution.py:50
  176.3 4.4 %fusion = bf16[768,1536]{0,1:T(8,128)(2,1)} fusion(bf16[512,1536]{1,0:T(8,128)(2,1)} %all-gather.3.cloned.1.call-done, bf16[512,768]{1,0:T(8,128)(2,1)} %copy-done.1), kind=kOutput, calls=%fused_computation.4 | convolution fusion | flops 1209139200 | bytes 4718592 | tf_op jit(solution)/shard_map/dot_general | solution.py:42
  180.8 4.3 %copy.9 = bf16[768,1536]{1,0:T(8,128)(2,1)} copy(bf16[768,1536]{0,1:T(8,128)(2,1)} %fusion) | data formatting | bytes 4718592
  185.0 27.0 %all-gather.5.cloned.1.call-done = bf16[512,1536]{1,0:T(8,128)(2,1)} async-done(((bf16[32,1536]{1,0:T(8,128)(2,1)}), bf16[512,1536]{1,0:T(8,128)(2,1)}) %all-gather.5.cloned.1.call-update) | async-done | bytes 1572880 | tf_op jit(solution)/shard_map/all_gather | solution.py:40
  212.0 4.2 %fusion.1 = bf16[768,1536]{0,1:T(8,128)(2,1)} fusion(bf16[512,1536]{1,0:T(8,128)(2,1)} %all-gather.5.cloned.1.call-done, bf16[512,768]{1,0:T(8,128)(2,1)S(1)} %all_gather.13), kind=kOutput, calls=%fused_computation.5 | convolution fusion | flops 1209139200 | bytes 4718592 | tf_op jit(solution)/shard_map/dot_general | solution.py:45
  216.2 4.3 %copy.10 = bf16[768,1536]{1,0:T(8,128)(2,1)} copy(bf16[768,1536]{0,1:T(8,128)(2,1)} %fusion.1) | data formatting | bytes 4718592
  220.5 2.3 convert_reduce_fusion
  222.8 68.0 %reduce-scatter.5.cloned.1.call-done = f32[32,768]{1,0:T(8,128)} async-done(((f32[512,768]{1,0:T(8,128)}), f32[32,768]{1,0:T(8,128)}) %reduce-scatter.5.cloned.1.call-update) | async-done | bytes 98320 | tf_op jit(solution)/shard_map/reduce_scatter | solution.py:49
  290.7 1.5 convert_element_type.29
  (8 shorter events, 0.1 us)
Async XLA Ops:
  7.2 42.2 %copy-start = (bf16[768,1536]{1,0:T(8,128)(2,1)S(1)}, bf16[768,1536]{1,0:T(8,128)(2,1)}, u32[]{:S(2)}) copy-start(bf16[768,1536]{1,0:T(8,128)(2,1)} %param.7) | copy-start | bytes 7077892
  7.2 121.3 %reduce-scatter.3.cloned.1.call-start = ((), (), s32[]{:S(2)}) async-start(), calls=%async_computation.2 | async-start | bytes 6684672 | tf_op jit(solution)/shard_map/reduce_scatter | solution.py:34
  46.0 3.4 %copy-start.1 = (bf16[512,768]{1,0:T(8,128)(2,1)}, bf16[512,768]{1,0:T(8,128)(2,1)S(1)}, u32[]{:S(2)}) copy-start(bf16[512,768]{1,0:T(8,128)(2,1)S(1)} %all_gather.12) | copy-start | bytes 2359300
  53.9 0.7 copy-start.2
  54.0 118.4 %all-gather.3.cloned.1.call-start = ((), (), s32[]{:S(2)}) async-start(), calls=%async_computation.3 | async-start | bytes 1671168 | tf_op jit(solution)/shard_map/all_gather | solution.py:39
  130.3 81.7 %all-gather.5.cloned.1.call-start = ((), (), s32[]{:S(2)}) async-start(), calls=%async_computation.5 | async-start | bytes 1671168 | tf_op jit(solution)/shard_map/all_gather | solution.py:40
  131.0 159.7 %reduce-scatter.5.cloned.1.call-start = ((), (), s32[]{:S(2)}) async-start(), calls=%async_computation.4 | async-start | bytes 1671168 | tf_op jit(solution)/shard_map/reduce_scatter | solution.py:49
Sparse Core Ops, SparseCore 0:
  54.1 74.3 reduce-scatter.2
  130.8 41.4 all-gather.2
  174.2 37.7 all-gather.4
  215.3 75.3 reduce-scatter.4
where the time goes:
time: 300 us; the launch traced here: 299 us
  waiting for transfers between devices  211 us (70%)
  blocking collectives  38.7 us (13%)
  matrix products  17.4 us (6%)
  between operations  13.8 us (5%)
  local copies, waits for them, and re-layouts  9.16 us (3%)
  other arithmetic  8.84 us (3%)
    reduce_scatter x1, waiting for transfers between devices, body(): lax.psum_scatter(jnp.concatenate([first, second], axis=1), 'row', scatter...  73.8 us
    reduce_scatter x1, waiting for transfers between devices, body(): lax.psum_scatter(lax.dot_general(full_grad, up_weight, (((1,), (1,)), (()...  68 us
    all_gather x1, waiting for transfers between devices, body(): lax.all_gather(act_grad, 'row', axis=0, tiled=True)  41.2 us
    all_gather x1, waiting for transfers between devices, body(): lax.all_gather(hidden_out, 'row', axis=0, tiled=True)  27 us
    all_gather x1, blocking collectives, body(): lax.all_gather(output_grad, 'col', axis=0, tiled=True)  20.4 us
    all_gather x1, blocking collectives, body(): lax.all_gather(activations, 'col', axis=0, tiled=True)  18.3 us
    unnamed x8, local copies, waits for them, and re-layouts  9.16 us
  transfers between devices with their start and end apart: 4, of which 4 were waited for; matrix products, arithmetic and copies ran while one was open for 8% of the time, Pallas kernels for 0%

commit v1 on v0

v1 whole, which is shorter than its diff:
```python
import functools

import jax
import jax.numpy as jnp
from jax import lax
from jax.experimental import pallas as pl
from jax.experimental.pallas import tpu as pltpu
from jax.sharding import PartitionSpec as P

MESH = pl.DeviceIdType.MESH
F32 = jnp.float32
BF16 = jnp.bfloat16

NZ = 8
R = 16
H = 768
TILE = 256
N_SEM = 220
N_LOCAL = 32


def gelu_parts(pre_act):
    coeff = 0.7978845608028654
    cubic = 0.044715
    inner = coeff * (pre_act + cubic * pre_act * pre_act * pre_act)
    tanh_val = jnp.tanh(inner)
    value = 0.5 * pre_act * (1.0 + tanh_val)
    slope = 0.5 * (1.0 + tanh_val) + 0.5 * pre_act * (1.0 - tanh_val * tanh_val) * coeff * (
        1.0 + 3.0 * cubic * pre_act * pre_act
    )
    return (value, slope)


def enc(v):
    return (v * jnp.abs(v)).astype(BF16)


def dec(code):
    v = code.astype(F32)
    root = jnp.sqrt(jnp.abs(v))
    return jnp.where(v < 0, -root, root)


def exchange_kernel(
    act_hbm, og_hbm, wu_hbm, wd_hbm, bias_ref,
    g_out, xt_out, ig_out,
    x_buf, wx, wu_other, part, sp, rp, sm, rm, g_buf, xt, ig_acc,
    s1, r1, t1, s2, r2, send_sem, recv_sem, local_sem,
):
    row, col = lax.axis_index("row"), lax.axis_index("col")
    z, core = row // 2, row % 2
    x, y = col // 4, col % 4
    par, yh = y % 2, y // 2

    sib = (z * 2 + 1 - core, col)
    zp = (((z + 1) % NZ) * 2 + core, col)
    zm = (((z + NZ - 1) % NZ) * 2 + core, col)

    def xpeer(k):
        return (row, ((x + k) % 4) * 4 + y)

    def ypeer(k):
        return (row, x * 4 + (y + k) % 4)

    sent, local = [], []
    count = {"remote": 0, "local": 0}

    def remote(src, dst, device):
        i = count["remote"]
        count["remote"] = i + 1
        copy = pltpu.make_async_remote_copy(
            src_ref=src, dst_ref=dst, send_sem=send_sem.at[i], recv_sem=recv_sem.at[i],
            device_id=device, device_id_type=MESH,
        )
        copy.start()
        sent.append(copy)
        return copy

    def move(src, dst):
        i = count["local"]
        count["local"] = i + 1
        copy = pltpu.make_async_copy(src, dst, local_sem.at[i])
        copy.start()
        return copy

    own_cols = pl.ds(pl.multiple_of(core * H, H), H)
    other_cols = pl.ds(pl.multiple_of((1 - core) * H, H), H)

    def xi(arr, whose, h):
        return arr * 4 + whose * 2 + h

    mine = {}
    for h in range(2):
        for arr, src in ((0, act_hbm), (1, og_hbm)):
            mine[arr, h] = move(src.at[pl.ds(h * R, R)], x_buf.at[xi(arr, 0, h), par, x, yh])
    w_own = [
        move(wu_hbm.at[:, own_cols], wx.at[0]),
        move(wd_hbm.at[:, own_cols], wx.at[2]),
    ]
    w_oth = move(wu_hbm.at[:, other_cols], wu_other)

    barrier = pltpu.get_barrier_semaphore()
    peers = [sib, zp, zm] + [xpeer(k) for k in (1, 2, 3)] + [ypeer(k) for k in (1, 2, 3)]
    for peer in peers:
        pl.semaphore_signal(barrier, inc=1, device_id=peer, device_id_type=MESH)
    pl.semaphore_wait(barrier, len(peers))

    stage1, stage2, shared = {}, {}, {}

    def gather1(h):
        for arr in (0, 1):
            mine[arr, h].wait()
        for k in (1, 2, 3):
            for arr, peer in ((0, xpeer(k)), (1, ypeer(k))):
                slot = x_buf.at[xi(arr, 0, h), par, x, yh]
                stage1[arr, h, k] = remote(slot, slot, peer)

    def group(arr, whose, h, k):
        if arr == 0:
            yk = (y + 4 - k) % 4
            return x_buf.at[xi(0, whose, h), yk % 2, :, yk // 2]
        return x_buf.at[xi(1, whose, h), :, (x + 4 - k) % 4]

    def share(arr, h, k):
        shared[arr, h, k] = remote(group(arr, 0, h, k), group(arr, 1, h, k), sib)

    def gather2(h):
        for k in (1, 2, 3):
            for arr in (0, 1):
                stage1[arr, h, k].wait_recv()
        for k in (1, 2, 3):
            for arr, peer in ((0, ypeer(k)), (1, xpeer(k))):
                slot = group(arr, 0, h, 0)
                stage2[arr, h, k] = remote(slot, slot, peer)
        for arr in (0, 1):
            share(arr, h, 0)

    def gather3(h):
        for k in (1, 3, 2):
            for arr in (0, 1):
                stage2[arr, h, k].wait_recv()
                share(arr, h, k)

    def gathered(h):
        for k in (0, 1, 3, 2):
            for arr in (0, 1):
                shared[arr, h, k].wait_recv()

    def project(h):
        for ab in (0, 1):
            lhs = [x_buf[xi(ab, w, h)].reshape(256, H) for w in (0, 1)]

            @pl.loop(0, H // TILE)
            def _(n):
                cols = pl.ds(pl.multiple_of(n * TILE, TILE), TILE)
                total = jnp.dot(lhs[0], wx[ab * 2, :, cols], preferred_element_type=F32)
                total += jnp.dot(lhs[1], wx[ab * 2 + 1, :, cols], preferred_element_type=F32)
                part[h * 2 + ab, :, :, :, cols] = total.reshape(2, NZ, R, TILE)

    up, down = {}, {}

    def reduce_step(q, s):
        h, p = q // 2, q % 2
        for way, hops, send_buf, recv_buf, device, first in (
            (1, up, sp, rp, zp, 0),
            (-1, down, sm, rm, zm, 1),
        ):
            owner = (z + NZ + way * (4 - s)) % NZ
            if s > 0:
                hops[q, s - 1].wait_recv()
            for ab in (0, 1):
                if s == 0 and ab != first:
                    continue
                v = part[h * 2 + ab, p, owner]
                if s > 1 or (s == 1 and ab == first):
                    v = v + dec(recv_buf[q * 4 + s - 1, ab])
                send_buf[q * 4 + s, ab] = enc(v)
            which = pl.ds(first, 1) if s == 0 else pl.ds(0, 2)
            hops[q, s] = remote(
                send_buf.at[q * 4 + s, which], recv_buf.at[q * 4 + s, which], device
            )

    fwd, bwd, pair = {}, {}, {}

    def to_sibling(q, i, owner):
        pair[q, i] = remote(g_buf.at[pl.ds(0, 2), q, owner], g_buf.at[pl.ds(2, 2), q, owner], sib)

    def finish(q):
        h, p = q // 2, q % 2
        up[q, 3].wait_recv()
        down[q, 3].wait_recv()
        both = [
            part[h * 2 + ab, p, z] + dec(rp[q * 4 + 3, ab]) + dec(rm[q * 4 + 3, ab])
            for ab in (0, 1)
        ]
        value, slope = gelu_parts(both[0] + bias_ref[core].astype(F32))
        g_buf[0, q, z] = (both[1] * slope).astype(BF16)
        g_buf[1, q, z] = value.astype(BF16)
        slot = g_buf.at[pl.ds(0, 2), q, z]
        fwd[q, 0] = remote(slot, slot, zp)
        bwd[q, 0] = remote(slot, slot, zm)
        to_sibling(q, 0, z)

    def spread_step(q, s):
        for way, hops, device, i in ((-1, fwd, zp, 0), (1, bwd, zm, 1)):
            owner = (z + NZ + way * s) % NZ
            hops[q, s - 1].wait_recv()
            slot = g_buf.at[pl.ds(i, 1) if s == 3 else pl.ds(0, 2), q, owner]
            hops[q, s] = remote(slot, slot, device)
            to_sibling(q, 2 * s - 1 + i, owner)

    def spread_last(q):
        fwd[q, 3].wait_recv()
        bwd[q, 3].wait_recv()
        to_sibling(q, 7, (z + 4) % NZ)

    def spread_done(q):
        for i in range(8):
            pair[q, i].wait_recv()
        local.append(move(g_buf.at[pl.ds(0, 2), q], g_out.at[:, q, :, :, own_cols]))
        local.append(move(g_buf.at[pl.ds(2, 2), q], g_out.at[:, q, :, :, other_cols]))

    near, far = {}, {}

    def backproject(h):
        grads = [g_buf[half * 2, pl.ds(2 * h, 2)].reshape(256, H) for half in (0, 1)]
        nt = (((1,), (1,)), ((), ()))

        @pl.loop(0, H // TILE)
        def _(n):
            rows = pl.ds(pl.multiple_of(n * TILE, TILE), TILE)
            total = lax.dot_general(grads[0], wx[0, rows], nt, preferred_element_type=F32)
            total += lax.dot_general(grads[1], wu_other[rows], nt, preferred_element_type=F32)
            ig_acc[h, :, :, :, :, rows] = total.reshape(2, 4, 2, R, TILE)

    halves = (pl.ds(0, H // 2), pl.ds(H // 2, H // 2))

    def rows_for(h, side, k):
        if side == 0:
            yk = (y + k) % 4
            return ig_acc[h, yk % 2, :, yk // 2, :, halves[0]]
        return ig_acc[h, :, (x + k) % 4, :, :, halves[1]].reshape(4, R, H // 2)

    def scatter1(h):
        for k in (2, 1, 3):
            for side in (0, 1):
                i = (h * 2 + side) * 3 + k - 1
                s1[i] = enc(rows_for(h, side, k))
                near[h, side, k] = remote(s1.at[i], r1.at[i], (ypeer, xpeer)[side](k))

    def scatter2(h):
        for side in (0, 1):
            total = rows_for(h, side, 0)
            for k in (1, 3, 2):
                near[h, side, k].wait_recv()
                total = total + dec(r1[(h * 2 + side) * 3 + k - 1])
            t1[side] = total
            for k in (2, 1, 3):
                i = (h * 2 + side) * 3 + k - 1
                if side == 0:
                    block = t1[0, (x + k) % 4]
                else:
                    yk = (y + k) % 4
                    block = t1[1, (yk % 2) * 2 + yk // 2]
                s2[i] = enc(block)
                far[h, side, k] = remote(s2.at[i], r2.at[i], (xpeer, ypeer)[side](k))

    def scatter3(h):
        for side in (0, 1):
            total = t1[0, x] if side == 0 else t1[1, par * 2 + yh]
            for k in (1, 3, 2):
                far[h, side, k].wait_recv()
                total = total + dec(r2[(h * 2 + side) * 3 + k - 1])
            ig_out[pl.ds(h * R, R), halves[side]] = total.astype(BF16)

    def transpose(arr):
        for h in (0, 1):
            xt[arr, :, h * 256 : (h + 1) * 256] = x_buf[xi(arr, 0, h)].reshape(256, H).T
        local.append(move(xt.at[arr], xt_out.at[arr]))

    gather1(0)
    w_sib = [
        remote(wu_hbm.at[:, other_cols], wx.at[1], sib),
        remote(wd_hbm.at[:, other_cols], wx.at[3], sib),
    ]
    gather2(0)
    gather1(1)
    gather3(0)
    gather2(1)
    for copy in w_own:
        copy.wait()
    for copy in w_sib:
        copy.wait_recv()
    gathered(0)
    project(0)
    reduce_step(0, 0)
    reduce_step(1, 0)
    reduce_step(0, 1)
    reduce_step(1, 1)
    gather3(1)
    reduce_step(0, 2)
    reduce_step(1, 2)
    gathered(1)
    project(1)
    reduce_step(2, 0)
    reduce_step(3, 0)
    reduce_step(0, 3)
    reduce_step(1, 3)
    reduce_step(2, 1)
    reduce_step(3, 1)
    finish(0)
    finish(1)
    reduce_step(2, 2)
    reduce_step(3, 2)
    spread_step(0, 1)
    spread_step(1, 1)
    reduce_step(2, 3)
    reduce_step(3, 3)
    spread_step(0, 2)
    spread_step(1, 2)
    finish(2)
    finish(3)
    spread_step(0, 3)
    spread_step(1, 3)
    transpose(0)
    spread_step(2, 1)
    spread_step(3, 1)
    spread_last(0)
    spread_last(1)
    transpose(1)
    spread_step(2, 2)
    spread_step(3, 2)
    spread_done(0)
    spread_done(1)
    w_oth.wait()
    backproject(0)
    scatter1(0)
    spread_step(2, 3)
    spread_step(3, 3)
    spread_last(2)
    spread_last(3)
    scatter2(0)
    spread_done(2)
    spread_done(3)
    backproject(1)
    scatter1(1)
    scatter3(0)
    scatter2(1)
    scatter3(1)
    for copy in sent:
        copy.wait_send()
    for copy in local:
        copy.wait()
    assert count["remote"] <= N_SEM and count["local"] <= N_LOCAL


def weight_kernel(g_ref, xt_ref, ig_ref, up_ref, down_ref, bias_ref, ig_out):
    width = g_ref.shape[-1]
    act_grad = g_ref[0].reshape(512, width)
    hidden = g_ref[1].reshape(512, width)
    up_ref[...] = jnp.dot(xt_ref[0], act_grad, preferred_element_type=F32).astype(BF16)
    down_ref[...] = jnp.dot(xt_ref[1], hidden, preferred_element_type=F32).astype(BF16)
    bias_ref[...] = jnp.sum(act_grad.astype(F32), axis=0, keepdims=True)
    ig_out[...] = ig_ref[...]


def body(activations, output_grad, up_weight, down_weight, up_bias):
    anywhere = pl.BlockSpec(memory_space=pl.ANY)
    vmem = pl.BlockSpec(memory_space=pltpu.VMEM)
    g, xt, ig = pl.pallas_call(
        exchange_kernel,
        out_shape=[
            jax.ShapeDtypeStruct((2, 4, NZ, R, 2 * H), BF16),
            jax.ShapeDtypeStruct((2, H, 512), BF16),
            jax.ShapeDtypeStruct((2 * R, H), BF16),
        ],
        in_specs=[anywhere] * 4 + [vmem],
        out_specs=[anywhere, anywhere, vmem],
        scratch_shapes=[
            pltpu.VMEM((8, 2, 4, 2, R, H), BF16),
            pltpu.VMEM((4, H, H), BF16),
            pltpu.VMEM((H, H), BF16),
            pltpu.VMEM((4, 2, NZ, R, H), F32),
            pltpu.VMEM((16, 2, R, H), BF16),
            pltpu.VMEM((16, 2, R, H), BF16),
            pltpu.VMEM((16, 2, R, H), BF16),
            pltpu.VMEM((16, 2, R, H), BF16),
            pltpu.VMEM((4, 4, NZ, R, H), BF16),
            pltpu.VMEM((2, H, 512), BF16),
            pltpu.VMEM((2, 2, 4, 2, R, H), F32),
            pltpu.VMEM((12, 4, R, H // 2), BF16),
            pltpu.VMEM((12, 4, R, H // 2), BF16),
            pltpu.VMEM((2, 4, R, H // 2), F32),
            pltpu.VMEM((12, R, H // 2), BF16),
            pltpu.VMEM((12, R, H // 2), BF16),
            pltpu.SemaphoreType.DMA((N_SEM,)),
            pltpu.SemaphoreType.DMA((N_SEM,)),
            pltpu.SemaphoreType.DMA((N_LOCAL,)),
        ],
        compiler_params=pltpu.CompilerParams(
            collective_id=0, has_side_effects=True, vmem_limit_bytes=56 << 20
        ),
        cost_estimate=pl.CostEstimate(
            flops=3 * 2 * 512 * H * 2 * H, bytes_accessed=12 << 20, transcendentals=64 * H
        ),
        name="exchange",
    )(activations, output_grad, up_weight, down_weight, up_bias.reshape(2, 1, H))
    tile = 256
    up_grad, down_grad, bias_grad, input_grad = pl.pallas_call(
        weight_kernel,
        grid=(2 * H // tile,),
        out_shape=[
            jax.ShapeDtypeStruct((H, 2 * H), BF16),
            jax.ShapeDtypeStruct((H, 2 * H), BF16),
            jax.ShapeDtypeStruct((1, 2 * H), F32),
            jax.ShapeDtypeStruct((2 * R, H), BF16),
        ],
        in_specs=[
            pl.BlockSpec((2, 4, NZ, R, tile), lambda n: (0, 0, 0, 0, n)),
            pl.BlockSpec((2, H, 512), lambda n: (0, 0, 0)),
            pl.BlockSpec((2 * R, H), lambda n: (0, 0)),
        ],
        out_specs=[
            pl.BlockSpec((H, tile), lambda n: (0, n)),
            pl.BlockSpec((H, tile), lambda n: (0, n)),
            pl.BlockSpec((1, tile), lambda n: (0, n)),
            pl.BlockSpec((2 * R, H), lambda n: (0, 0)),
        ],
        compiler_params=pltpu.CompilerParams(vmem_limit_bytes=40 << 20),
        cost_estimate=pl.CostEstimate(
            flops=2 * 2 * 512 * H * 2 * H, bytes_accessed=10 << 20, transcendentals=0
        ),
        name="weight_grads",
    )(g, xt, ig)
    return (input_grad, up_grad, down_grad, bias_grad.reshape(2 * H))


def solution(mesh):
    placed = (P("col", "row"), P("col", "row"), P("row", "col"), P("row", "col"), P("col"))
    return jax.shard_map(
        body,
        mesh=mesh,
        in_specs=placed,
        out_specs=(P("col", "row"), P("row", "col"), P("row", "col"), P("col")),
        check_vma=False,
    )
```

time: 300 us -> 91.8 us (0.31)
  waiting for transfers between devices: 211 us -> 0 us
  Pallas kernels: 0 us -> 84.9 us
  blocking collectives: 38.7 us -> 0 us
  matrix products: 17.4 us -> 0 us
  between operations: 13.8 us -> 0.65 us
  other arithmetic: 8.84 us -> 0.62 us
  local copies, waits for them, and re-layouts: 9.16 us -> 5.38 us
    reduce_scatter x2 -> x0, waiting for transfers between devices: 142 us -> none  [the longest x1 73.8 us: body(): lax.psum_scatter(jnp.concatenate([first, second], axis=1), 'row', scatter...]
    pallas_call x0 -> x2, Pallas kernels: none -> 84.9 us  [the longest x1 79.8 us: body(): pl.pallas_call(exchange_kernel, out_shape=[jax.ShapeDtypeStruct((2, 4, NZ...]
    all_gather x2 -> x0, waiting for transfers between devices: 68.2 us -> none  [the longest x1 41.2 us: body(): lax.all_gather(act_grad, 'row', axis=0, tiled=True)]
    all_gather x2 -> x0, blocking collectives: 38.7 us -> none  [the longest x1 20.4 us: body(): lax.all_gather(output_grad, 'col', axis=0, tiled=True)]
    dot_general x5 -> x0, matrix products: 17.4 us -> none  [the longest x1 4.44 us: body(): lax.dot_general(seen_acts, full_grad, (((0,), (0,)), ((), ())), preferred...]
    unnamed x8 -> x6, local copies, waits for them, and re-layouts: 9.16 us -> 4.09 us
    convert_element_type x3 -> x0, other arithmetic: 3.35 us -> none  [the longest x1 1.83 us: finish(): value.astype(jnp.bfloat16)]
    concatenate x1 -> x0, other arithmetic: 3.22 us -> none  [body(): jnp.concatenate([first, second], axis=1)]
  transfers between devices with their start and end apart: 4 -> 0, of which waited for: 4 -> 0; matrix products, arithmetic and copies ran while one was open for 8% -> 0% of each run, Pallas kernels for 0% -> 0%
where the time goes in v1:
time: 91.8 us; the launch traced here: 91.6 us
  Pallas kernels  84.9 us (92%)
  local copies, waits for them, and re-layouts  5.38 us (6%)
    pallas_call x1, Pallas kernels, body(): pl.pallas_call(exchange_kernel, out_shape=[jax.ShapeDtypeStruct((2, 4, NZ...  79.8 us
    pallas_call x1, Pallas kernels, body(): pl.pallas_call(weight_kernel, grid=(2 * H // tile,), out_shape=[jax.Shape...  5.12 us
    unnamed x6, local copies, waits for them, and re-layouts  4.09 us

profile of v1, /device:TPU:1, one launch (start us, length us, event | category | flops | bytes accessed | tf_op | source)
XLA Modules:
  0.0 91.6 jit_solution(11161695058156378646)
XLA Ops:
  0.6 1.3 %reshape.16.bias_ref = bf16[2,1,768]{2,1,0:T(2,128)(2,1)} reshape(bf16[1536]{0:T(1024)(128)(2,1)} %param.9) | data formatting | bytes 6144 | tf_op jit(solution)/shard_map/reshape | solution.py:407
  1.9 79.8 %exchange.1 = (bf16[2,4,8,16,1536]{4,3,2,1,0:T(8,128)(2,1)}, bf16[2,768,512]{2,1,0:T(8,128)(2,1)}, bf16[32,768]{1,0:T(8,128)(2,1)}) custom-call(bf16[32,768]{1,0:T(8,128)(2,1)} %act_hbm.1, bf16[32,768]{1,0:T(8,128)(2,1)} %og_hbm.1, bf16[768,1536]{1,0:T(8,128)(2,1)} %wu_hbm.1, bf16[768,1536]{1,0:T(8,128)(2,1)} %wd_hbm.1, bf16[2,1,768]{2,1,0:T(2,128)(2,1)} %reshape.16.bias_ref), custom_call_target="tpu_custom_call" | custom-call | flops 3623878656 | bytes 12582912 | tf_op jit(solution)/shard_map/exchange/pallas_call | solution.py:370
  81.7 0.0 copy-start
  81.7 1.9 %copy-done = bf16[2,4,8,16,1536]{4,3,2,1,0:T(8,128)(2,1)S(1)} copy-done((bf16[2,4,8,16,1536]{4,3,2,1,0:T(8,128)(2,1)S(1)}, bf16[2,4,8,16,1536]{4,3,2,1,0:T(8,128)(2,1)}, u32[]{:S(2)}) %copy-start) | copy-done | bytes 3145752
  83.6 0.0 copy-start.1
  83.6 1.4 %copy-done.1 = bf16[2,768,512]{2,1,0:T(8,128)(2,1)S(1)} copy-done((bf16[2,768,512]{2,1,0:T(8,128)(2,1)S(1)}, bf16[2,768,512]{2,1,0:T(8,128)(2,1)}, u32[]{:S(2)}) %copy-start.1) | copy-done | bytes 1572888
  85.0 0.0 copy-start.2
  85.0 0.8 copy-done.2
  85.8 5.1 %weight_grads.1 = (bf16[768,1536]{1,0:T(8,128)(2,1)}, bf16[768,1536]{1,0:T(8,128)(2,1)}, f32[1,1536]{1,0:T(1,128)S(1)}, bf16[32,768]{1,0:T(8,128)(2,1)}) custom-call(bf16[2,4,8,16,1536]{4,3,2,1,0:T(8,128)(2,1)S(1)} %copy-done, bf16[2,768,512]{2,1,0:T(8,128)(2,1)S(1)} %copy-done.1, bf16[32,768]{1,0:T(8,128)(2,1)S(1)} %copy-done.2), custom_call_target="tpu_custom_call" | custom-call | flops 2415919104 | bytes 10485760 | tf_op jit(solution)/shard_map/weight_grads/pallas_call | solution.py:409
  90.9 0.6 reduce
Async XLA Ops:
  81.7 1.9 %copy-start = (bf16[2,4,8,16,1536]{4,3,2,1,0:T(8,128)(2,1)S(1)}, bf16[2,4,8,16,1536]{4,3,2,1,0:T(8,128)(2,1)}, u32[]{:S(2)}) copy-start(bf16[2,4,8,16,1536]{4,3,2,1,0:T(8,128)(2,1)} %get-tuple-element.11.g_ref) | copy-start | bytes 9437188
  83.6 1.4 %copy-start.1 = (bf16[2,768,512]{2,1,0:T(8,128)(2,1)S(1)}, bf16[2,768,512]{2,1,0:T(8,128)(2,1)}, u32[]{:S(2)}) copy-start(bf16[2,768,512]{2,1,0:T(8,128)(2,1)} %get-tuple-element.12.xt_ref) | copy-start | bytes 4718596
  85.0 0.8 copy-start.2

commit v2 on v1

v2 whole, which is shorter than its diff:
```python
import functools

import jax
import jax.numpy as jnp
from jax import lax
from jax.experimental import pallas as pl
from jax.experimental.pallas import tpu as pltpu
from jax.sharding import PartitionSpec as P

MESH = pl.DeviceIdType.MESH
F32 = jnp.float32
BF16 = jnp.bfloat16

NZ = 8
R = 16
H = 768
TILE = 256

S_GATHER1, S_GATHER2, S_SHARE, S_WEIGHTS, S_CHAIN, S_PAIR, S_NEAR, S_FAR, N_SEND = range(9)
R_GATHER1, R_GATHER2, R_SHARE, R_WEIGHTS, R_CHAIN, R_PAIR, R_NEAR, R_FAR, N_RECV = (
    0, 2, 14, 16, 17, 33, 37, 41, 45,
)
L_IN, L_UP, L_DOWN, L_OTHER, L_BIAS, L_G, L_XT, L_IG, N_LOCAL = 0, 2, 3, 4, 5, 6, 7, 8, 9


def gelu_parts(pre_act):
    coeff = 0.7978845608028654
    cubic = 0.044715
    inner = coeff * (pre_act + cubic * pre_act * pre_act * pre_act)
    tanh_val = jnp.tanh(inner)
    value = 0.5 * pre_act * (1.0 + tanh_val)
    slope = 0.5 * (1.0 + tanh_val) + 0.5 * pre_act * (1.0 - tanh_val * tanh_val) * coeff * (
        1.0 + 3.0 * cubic * pre_act * pre_act
    )
    return (value, slope)


def enc(v):
    return (v * jnp.abs(v)).astype(BF16)


def dec(code):
    v = code.astype(F32)
    root = jnp.sqrt(jnp.abs(v))
    return jnp.where(v < 0, -root, root)


def exchange_kernel(
    act_hbm, og_hbm, wu_hbm, wd_hbm, bias_hbm,
    g_out, xt_out, ig_hbm,
    x_buf, wx, wu_other, part, sp, rp, sm, rm, g_buf, xt, ig_acc,
    s1, r1, t1, s2, r2, bias_buf, ig_out, send_sem, recv_sem, local_sem,
):
    row, col = lax.axis_index("row"), lax.axis_index("col")
    z, core = row // 2, row % 2
    x, y = col // 4, col % 4
    par, yh = y % 2, y // 2

    sib = (z * 2 + 1 - core, col)
    zp = (((z + 1) % NZ) * 2 + core, col)
    zm = (((z + NZ - 1) % NZ) * 2 + core, col)

    def xpeer(k):
        return (row, ((x + k) % 4) * 4 + y)

    def ypeer(k):
        return (row, x * 4 + (y + k) % 4)

    def remote(src, dst, device, sent, received):
        copy = pltpu.make_async_remote_copy(
            src_ref=src, dst_ref=dst, send_sem=send_sem.at[sent], recv_sem=recv_sem.at[received],
            device_id=device, device_id_type=MESH,
        )
        copy.start()
        return copy

    def move(src, dst, i):
        copy = pltpu.make_async_copy(src, dst, local_sem.at[i])
        copy.start()
        return copy

    def wait_for(ref, sem):
        pltpu.make_async_copy(ref, ref, sem).wait()

    own_cols = pl.ds(pl.multiple_of(core * H, H), H)
    other_cols = pl.ds(pl.multiple_of((1 - core) * H, H), H)

    def xi(arr, whose, h):
        return arr * 4 + whose * 2 + h

    for h in range(2):
        for arr, src in ((0, act_hbm), (1, og_hbm)):
            move(src.at[pl.ds(h * R, R)], x_buf.at[xi(arr, 0, h), par, x, yh], L_IN + h)
    weights = [
        move(wu_hbm.at[:, own_cols], wx.at[0], L_UP),
        move(wd_hbm.at[:, own_cols], wx.at[2], L_DOWN),
        move(wu_hbm.at[:, other_cols], wu_other, L_OTHER),
        move(bias_hbm, bias_buf, L_BIAS),
    ]

    barrier = pltpu.get_barrier_semaphore()
    peers = [sib, zp, zm] + [xpeer(k) for k in (1, 2, 3)] + [ypeer(k) for k in (1, 2, 3)]
    for peer in peers:
        pl.semaphore_signal(barrier, inc=1, device_id=peer, device_id_type=MESH)
    pl.semaphore_wait(barrier, len(peers))

    stage2 = {}

    def gather1(h):
        wait_for(x_buf.at[0, 0, 0], local_sem.at[L_IN + h])
        for k in (2, 1, 3):
            for arr, peer in ((0, xpeer(k)), (1, ypeer(k))):
                slot = x_buf.at[xi(arr, 0, h), par, x, yh]
                remote(slot, slot, peer, S_GATHER1, R_GATHER1 + h)

    def group(arr, whose, h, k):
        if arr == 0:
            yk = (y + 4 - k) % 4
            return x_buf.at[xi(0, whose, h), yk % 2, :, yk // 2]
        return x_buf.at[xi(1, whose, h), :, (x + 4 - k) % 4]

    def share(arr, h, k):
        remote(group(arr, 0, h, k), group(arr, 1, h, k), sib, S_SHARE, R_SHARE + h)

    def gather2(h):
        wait_for(x_buf.at[0, 0, pl.ds(0, 3)], recv_sem.at[R_GATHER1 + h])
        for k in (2, 1, 3):
            for arr, peer in ((0, ypeer(k)), (1, xpeer(k))):
                slot = group(arr, 0, h, 0)
                i = R_GATHER2 + (h * 2 + arr) * 3 + k - 1
                stage2[arr, h, k] = remote(slot, slot, peer, S_GATHER2, i)
        for arr in (0, 1):
            share(arr, h, 0)

    def gather3(h):
        for k in (1, 3, 2):
            for arr in (0, 1):
                stage2[arr, h, k].wait_recv()
                share(arr, h, k)

    def gathered(h):
        wait_for(x_buf.at[pl.ds(0, 2)], recv_sem.at[R_SHARE + h])

    def send_weights():
        remote(wu_hbm.at[:, other_cols], wx.at[1], sib, S_WEIGHTS, R_WEIGHTS)
        remote(wd_hbm.at[:, other_cols], wx.at[3], sib, S_WEIGHTS, R_WEIGHTS)

    def own_weights_ready():
        for copy in weights:
            copy.wait()

    def weights_ready():
        wait_for(wx.at[pl.ds(0, 2)], recv_sem.at[R_WEIGHTS])

    def project(h, whose):
        for ab in (0, 1):
            lhs = x_buf[xi(ab, whose, h)].reshape(256, H)

            @pl.loop(0, H // TILE)
            def _(n):
                cols = pl.ds(pl.multiple_of(n * TILE, TILE), TILE)
                total = jnp.dot(lhs, wx[ab * 2 + whose, :, cols], preferred_element_type=F32)
                total = total.reshape(2, NZ, R, TILE)
                if whose == 1:
                    total += part[h * 2 + ab, :, :, :, cols]
                part[h * 2 + ab, :, :, :, cols] = total

    up, down = {}, {}

    def chain_sem(q, way, step):
        return R_CHAIN + q * 4 + way * 2 + step % 2

    def reduce_step(q, s):
        h, p = q // 2, q % 2
        if s > 0:
            up[q, s - 1].wait_recv()
            down[q, s - 1].wait_recv()
        for way, hops, send_buf, recv_buf, device in ((0, up, sp, rp, zp), (1, down, sm, rm, zm)):
            first = way
            owner = (z + 4 - s) % NZ if way == 0 else (z + 4 + s) % NZ
            for ab in (0, 1):
                if s == 0 and ab != first:
                    continue
                v = part[h * 2 + ab, p, owner]
                if s > 1 or (s == 1 and ab == first):
                    v = v + dec(recv_buf[q * 4 + s - 1, ab])
                send_buf[q * 4 + s, ab] = enc(v)
            which = pl.ds(first, 1) if s == 0 else pl.ds(0, 2)
            hops[q, s] = remote(
                send_buf.at[q * 4 + s, which], recv_buf.at[q * 4 + s, which], device,
                S_CHAIN, chain_sem(q, way, s),
            )

    fwd, bwd = {}, {}

    def to_sibling(q, owner):
        remote(
            g_buf.at[pl.ds(0, 2), q, owner], g_buf.at[pl.ds(2, 2), q, owner], sib,
            S_PAIR, R_PAIR + q,
        )

    def finish(q):
        h, p = q // 2, q % 2
        up[q, 3].wait_recv()
        down[q, 3].wait_recv()
        both = [
            part[h * 2 + ab, p, z] + dec(rp[q * 4 + 3, ab]) + dec(rm[q * 4 + 3, ab])
            for ab in (0, 1)
        ]
        bias = bias_buf[...].astype(F32).reshape(1, 2 * H)
        bias = jnp.where(core == 0, bias[:, :H], bias[:, H:])
        value, slope = gelu_parts(both[0] + bias)
        g_buf[0, q, z] = (both[1] * slope).astype(BF16)
        g_buf[1, q, z] = value.astype(BF16)
        slot = g_buf.at[pl.ds(0, 2), q, z]
        fwd[q, 0] = remote(slot, slot, zp, S_CHAIN, chain_sem(q, 0, 0))
        bwd[q, 0] = remote(slot, slot, zm, S_CHAIN, chain_sem(q, 1, 0))
        to_sibling(q, z)

    def spread_step(q, s):
        fwd[q, s - 1].wait_recv()
        bwd[q, s - 1].wait_recv()
        owners = ((z + NZ - s) % NZ, (z + s) % NZ)
        for i, hops, device in ((0, fwd, zp), (1, bwd, zm)):
            slot = g_buf.at[pl.ds(i, 1) if s == 3 else pl.ds(0, 2), q, owners[i]]
            hops[q, s] = remote(slot, slot, device, S_CHAIN, chain_sem(q, i, s))
        for owner in owners:
            to_sibling(q, owner)

    def spread_last(q):
        fwd[q, 3].wait_recv()
        bwd[q, 3].wait_recv()
        to_sibling(q, (z + 4) % NZ)

    def spread_done(q):
        wait_for(g_buf.at[pl.ds(0, 2), q], recv_sem.at[R_PAIR + q])
        move(g_buf.at[pl.ds(0, 2), q], g_out.at[:, q, :, :, own_cols], L_G)
        move(g_buf.at[pl.ds(2, 2), q], g_out.at[:, q, :, :, other_cols], L_G)

    def backproject(h):
        grads = [g_buf[half * 2, pl.ds(2 * h, 2)].reshape(256, H) for half in (0, 1)]
        nt = (((1,), (1,)), ((), ()))

        @pl.loop(0, H // TILE)
        def _(n):
            rows = pl.ds(pl.multiple_of(n * TILE, TILE), TILE)
            total = lax.dot_general(grads[0], wx[0, rows], nt, preferred_element_type=F32)
            total += lax.dot_general(grads[1], wu_other[rows], nt, preferred_element_type=F32)
            ig_acc[h, :, :, :, :, rows] = total.reshape(2, 4, 2, R, TILE)

    halves = (pl.ds(0, H // 2), pl.ds(H // 2, H // 2))

    def rows_for(h, side, k):
        if side == 0:
            yk = (y + k) % 4
            return ig_acc[h, yk % 2, :, yk // 2, :, halves[0]]
        return ig_acc[h, :, (x + k) % 4, :, :, halves[1]].reshape(4, R, H // 2)

    def scatter1(h):
        for k in (2, 1, 3):
            for side in (0, 1):
                i = (h * 2 + side) * 3 + k - 1
                s1[i] = enc(rows_for(h, side, k))
                remote(
                    s1.at[i], r1.at[i], (ypeer, xpeer)[side](k), S_NEAR, R_NEAR + h * 2 + side
                )

    def scatter2(h):
        for side in (0, 1):
            total = rows_for(h, side, 0)
            wait_for(r1.at[pl.ds(0, 3)], recv_sem.at[R_NEAR + h * 2 + side])
            for k in (1, 3, 2):
                total = total + dec(r1[(h * 2 + side) * 3 + k - 1])
            t1[side] = total
            for k in (2, 1, 3):
                i = (h * 2 + side) * 3 + k - 1
                if side == 0:
                    block = t1[0, (x + k) % 4]
                else:
                    yk = (y + k) % 4
                    block = t1[1, (yk % 2) * 2 + yk // 2]
                s2[i] = enc(block)
                remote(
                    s2.at[i], r2.at[i], (xpeer, ypeer)[side](k), S_FAR, R_FAR + h * 2 + side
                )

    def scatter3(h):
        for side in (0, 1):
            total = t1[0, x] if side == 0 else t1[1, par * 2 + yh]
            wait_for(r2.at[pl.ds(0, 3)], recv_sem.at[R_FAR + h * 2 + side])
            for k in (1, 3, 2):
                total = total + dec(r2[(h * 2 + side) * 3 + k - 1])
            ig_out[pl.ds(h * R, R), halves[side]] = total.astype(BF16)
        move(ig_out.at[pl.ds(h * R, R)], ig_hbm.at[pl.ds(h * R, R)], L_IG)

    def transpose(arr):
        for h in (0, 1):
            xt[arr, :, h * 256 : (h + 1) * 256] = x_buf[xi(arr, 0, h)].reshape(256, H).T
        move(xt.at[arr], xt_out.at[arr], L_XT)

    def drain():
        for ref, i in (
            (x_buf.at[0, :, pl.ds(0, 3)], S_GATHER1),
            (x_buf.at[pl.ds(0, 3)], S_GATHER2),
            (x_buf.at[pl.ds(0, 4)], S_SHARE),
            (wx.at[pl.ds(0, 2)], S_WEIGHTS),
            (g_buf.at[:, :, pl.ds(0, 7)], S_CHAIN),
            (g_buf.at[pl.ds(0, 2)], S_PAIR),
            (s1, S_NEAR),
            (s2, S_FAR),
        ):
            wait_for(ref, send_sem.at[i])
        for ref, i in ((g_buf, L_G), (xt, L_XT), (ig_out, L_IG)):
            wait_for(ref, local_sem.at[i])

    gather1(0)
    send_weights()
    gather2(0)
    gather1(1)
    gather3(0)
    gather2(1)
    own_weights_ready()
    project(0, 0)
    weights_ready()
    gathered(0)
    project(0, 1)
    reduce_step(0, 0)
    reduce_step(1, 0)
    reduce_step(0, 1)
    reduce_step(1, 1)
    gather3(1)
    project(1, 0)
    reduce_step(0, 2)
    reduce_step(1, 2)
    gathered(1)
    project(1, 1)
    reduce_step(2, 0)
    reduce_step(3, 0)
    reduce_step(0, 3)
    reduce_step(1, 3)
    reduce_step(2, 1)
    reduce_step(3, 1)
    finish(0)
    finish(1)
    reduce_step(2, 2)
    reduce_step(3, 2)
    spread_step(0, 1)
    spread_step(1, 1)
    reduce_step(2, 3)
    reduce_step(3, 3)
    spread_step(0, 2)
    spread_step(1, 2)
    finish(2)
    finish(3)
    spread_step(0, 3)
    spread_step(1, 3)
    transpose(0)
    spread_step(2, 1)
    spread_step(3, 1)
    spread_last(0)
    spread_last(1)
    transpose(1)
    spread_step(2, 2)
    spread_step(3, 2)
    spread_done(0)
    spread_done(1)
    backproject(0)
    scatter1(0)
    spread_step(2, 3)
    spread_step(3, 3)
    spread_last(2)
    spread_last(3)
    scatter2(0)
    spread_done(2)
    spread_done(3)
    backproject(1)
    scatter1(1)
    scatter3(0)
    scatter2(1)
    scatter3(1)
    drain()


def weight_kernel(g_ref, xt_ref, ig_ref, up_ref, down_ref, bias_ref, ig_out):
    width = g_ref.shape[-1]
    act_grad = g_ref[0].reshape(512, width)
    hidden = g_ref[1].reshape(512, width)
    up_ref[...] = jnp.dot(xt_ref[0], act_grad, preferred_element_type=F32).astype(BF16)
    down_ref[...] = jnp.dot(xt_ref[1], hidden, preferred_element_type=F32).astype(BF16)
    start = pl.multiple_of(pl.program_id(0) * width, width)
    bias_ref[pl.ds(start, width)] = jnp.sum(act_grad.astype(F32), axis=0)
    ig_out[...] = ig_ref[...]


def body(activations, output_grad, up_weight, down_weight, up_bias):
    anywhere = pl.BlockSpec(memory_space=pl.ANY)
    g, xt, ig = pl.pallas_call(
        exchange_kernel,
        out_shape=[
            jax.ShapeDtypeStruct((2, 4, NZ, R, 2 * H), BF16),
            jax.ShapeDtypeStruct((2, H, 512), BF16),
            jax.ShapeDtypeStruct((2 * R, H), BF16),
        ],
        in_specs=[anywhere] * 5,
        out_specs=[anywhere] * 3,
        scratch_shapes=[
            pltpu.VMEM((8, 2, 4, 2, R, H), BF16),
            pltpu.VMEM((4, H, H), BF16),
            pltpu.VMEM((H, H), BF16),
            pltpu.VMEM((4, 2, NZ, R, H), F32),
            pltpu.VMEM((16, 2, R, H), BF16),
            pltpu.VMEM((16, 2, R, H), BF16),
            pltpu.VMEM((16, 2, R, H), BF16),
            pltpu.VMEM((16, 2, R, H), BF16),
            pltpu.VMEM((4, 4, NZ, R, H), BF16),
            pltpu.VMEM((2, H, 512), BF16),
            pltpu.VMEM((2, 2, 4, 2, R, H), F32),
            pltpu.VMEM((12, 4, R, H // 2), BF16),
            pltpu.VMEM((12, 4, R, H // 2), BF16),
            pltpu.VMEM((2, 4, R, H // 2), F32),
            pltpu.VMEM((12, R, H // 2), BF16),
            pltpu.VMEM((12, R, H // 2), BF16),
            pltpu.VMEM((2 * H,), BF16),
            pltpu.VMEM((2 * R, H), BF16),
            pltpu.SemaphoreType.DMA((N_SEND,)),
            pltpu.SemaphoreType.DMA((N_RECV,)),
            pltpu.SemaphoreType.DMA((N_LOCAL,)),
        ],
        compiler_params=pltpu.CompilerParams(
            collective_id=0, has_side_effects=True, vmem_limit_bytes=56 << 20
        ),
        cost_estimate=pl.CostEstimate(
            flops=3 * 2 * 512 * H * 2 * H, bytes_accessed=12 << 20, transcendentals=64 * H
        ),
        name="exchange",
    )(activations, output_grad, up_weight, down_weight, up_bias)
    tile = 256
    up_grad, down_grad, bias_grad, input_grad = pl.pallas_call(
        weight_kernel,
        grid=(2 * H // tile,),
        out_shape=[
            jax.ShapeDtypeStruct((H, 2 * H), BF16),
            jax.ShapeDtypeStruct((H, 2 * H), BF16),
            jax.ShapeDtypeStruct((2 * H,), F32),
            jax.ShapeDtypeStruct((2 * R, H), BF16),
        ],
        in_specs=[
            pl.BlockSpec((2, 4, NZ, R, tile), lambda n: (0, 0, 0, 0, n)),
            pl.BlockSpec((2, H, 512), lambda n: (0, 0, 0)),
            pl.BlockSpec((2 * R, H), lambda n: (0, 0)),
        ],
        out_specs=[
            pl.BlockSpec((H, tile), lambda n: (0, n)),
            pl.BlockSpec((H, tile), lambda n: (0, n)),
            pl.BlockSpec((2 * H,), lambda n: (0,)),
            pl.BlockSpec((2 * R, H), lambda n: (0, 0)),
        ],
        compiler_params=pltpu.CompilerParams(vmem_limit_bytes=60 << 20),
        cost_estimate=pl.CostEstimate(
            flops=2 * 2 * 512 * H * 2 * H, bytes_accessed=10 << 20, transcendentals=0
        ),
        name="weight_grads",
    )(g, xt, ig)
    return (input_grad, up_grad, down_grad, bias_grad)


def solution(mesh):
    placed = (P("col", "row"), P("col", "row"), P("row", "col"), P("row", "col"), P("col"))
    return jax.shard_map(
        body,
        mesh=mesh,
        in_specs=placed,
        out_specs=(P("col", "row"), P("row", "col"), P("row", "col"), P("col")),
        check_vma=False,
    )
```

time: 91.8 us -> 85.2 us (0.928)
  local copies, waits for them, and re-layouts: 5.38 us -> 0 us
    unnamed x6 -> x0, local copies, waits for them, and re-layouts: 4.09 us -> none
    pallas_call x1, Pallas kernels: 79.8 us -> 76.8 us  [body(): pl.pallas_call(exchange_kernel, out_shape=[jax.ShapeDtypeStruct((2, 4, NZ...]
    pallas_call x1, Pallas kernels: 5.12 us -> 7.54 us  [body(): pl.pallas_call(weight_kernel, grid=(2 * H // tile,), out_shape=[jax.Shape...]
    reshape x1 -> x0, local copies, waits for them, and re-layouts: 1.29 us -> none  [body(): up_bias.reshape(2, 1, H)]
where the time goes in v2:
time: 85.2 us; the launch traced here: 85 us
  Pallas kernels  84.3 us (99%)
    pallas_call x1, Pallas kernels, body(): pl.pallas_call(exchange_kernel, out_shape=[jax.ShapeDtypeStruct((2, 4, NZ...  76.8 us
    pallas_call x1, Pallas kernels, body(): pl.pallas_call(weight_kernel, grid=(2 * H // tile,), out_shape=[jax.Shape...  7.54 us

profile of v2, /device:TPU:1, one launch (start us, length us, event | category | flops | bytes accessed | tf_op | source)
XLA Modules:
  0.0 85.0 jit_solution(2442091201523647391)
XLA Ops:
  0.6 76.8 %exchange.1 = (bf16[2,4,8,16,1536]{4,3,2,1,0:T(8,128)(2,1)}, bf16[2,768,512]{2,1,0:T(8,128)(2,1)}, bf16[32,768]{1,0:T(8,128)(2,1)}) custom-call(bf16[32,768]{1,0:T(8,128)(2,1)} %act_hbm.1, bf16[32,768]{1,0:T(8,128)(2,1)} %og_hbm.1, bf16[768,1536]{1,0:T(8,128)(2,1)} %wu_hbm.1, bf16[768,1536]{1,0:T(8,128)(2,1)} %wd_hbm.1, bf16[1536]{0:T(1024)(128)(2,1)} %bias_hbm.1), custom_call_target="tpu_custom_call" | custom-call | flops 3623878656 | bytes 12582912 | tf_op jit(solution)/shard_map/exchange/pallas_call | solution.py:397
  77.4 7.5 %weight_grads.1 = (bf16[768,1536]{1,0:T(8,128)(2,1)}, bf16[768,1536]{1,0:T(8,128)(2,1)}, f32[1536]{0:T(1024)}, bf16[32,768]{1,0:T(8,128)(2,1)}) custom-call(bf16[2,4,8,16,1536]{4,3,2,1,0:T(8,128)(2,1)} %get-tuple-element.11.g_ref, bf16[2,768,512]{2,1,0:T(8,128)(2,1)} %get-tuple-element.12.xt_ref, bf16[32,768]{1,0:T(8,128)(2,1)} %get-tuple-element.13.ig_ref), custom_call_target="tpu_custom_call" | custom-call | flops 2415919104 | bytes 10485760 | tf_op jit(solution)/shard_map/weight_grads/pallas_call | solution.py:438

commit v3 on v2

v3 whole, which is shorter than its diff:
```python
import functools

import jax
import jax.numpy as jnp
from jax import lax
from jax.experimental import pallas as pl
from jax.experimental.pallas import tpu as pltpu
from jax.sharding import PartitionSpec as P

MESH = pl.DeviceIdType.MESH
F32 = jnp.float32
BF16 = jnp.bfloat16

NZ = 8
R = 16
H = 768
HALF = H // 2

S_GATHER1, S_GATHER2, S_SHARE, S_WEIGHTS, S_CHAIN, S_PAIR, S_NEAR, S_FAR, N_SEND = range(9)
R_GATHER1, R_GATHER2, R_SHARE, R_WEIGHTS, R_CHAIN, R_PAIR, R_NEAR, R_FAR, N_RECV = (
    0, 2, 14, 16, 17, 49, 53, 57, 61,
)
L_IN, L_UP, L_DOWN, L_OTHER, L_BIAS, N_LOCAL = 0, 2, 3, 4, 5, 6


def gelu_parts(pre_act):
    coeff = 0.7978845608028654
    cubic = 0.044715
    inner = coeff * (pre_act + cubic * pre_act * pre_act * pre_act)
    tanh_val = jnp.tanh(inner)
    value = 0.5 * pre_act * (1.0 + tanh_val)
    slope = 0.5 * (1.0 + tanh_val) + 0.5 * pre_act * (1.0 - tanh_val * tanh_val) * coeff * (
        1.0 + 3.0 * cubic * pre_act * pre_act
    )
    return (value, slope)


def enc(v):
    return (v * jnp.abs(v)).astype(BF16)


def dec(code):
    v = code.astype(F32)
    root = jnp.sqrt(jnp.abs(v))
    return jnp.where(v < 0, -root, root)


def exchange_kernel(
    act_hbm, og_hbm, wu_hbm, wd_hbm, bias_hbm,
    up_out, down_out, bias_out, ig_out,
    x_buf, wx, wu_other, part, sp, rp, sm, rm, g_buf, ig_acc,
    s1, r1, t1, s2, r2, bias_buf, send_sem, recv_sem, local_sem,
):
    row, col = lax.axis_index("row"), lax.axis_index("col")
    z, core = row // 2, row % 2
    x, y = col // 4, col % 4
    par, yh = y % 2, y // 2

    sib = (z * 2 + 1 - core, col)
    zp = (((z + 1) % NZ) * 2 + core, col)
    zm = (((z + NZ - 1) % NZ) * 2 + core, col)

    def xpeer(k):
        return (row, ((x + k) % 4) * 4 + y)

    def ypeer(k):
        return (row, x * 4 + (y + k) % 4)

    def remote(src, dst, device, sent, received):
        copy = pltpu.make_async_remote_copy(
            src_ref=src, dst_ref=dst, send_sem=send_sem.at[sent], recv_sem=recv_sem.at[received],
            device_id=device, device_id_type=MESH,
        )
        copy.start()
        return copy

    def move(src, dst, i):
        copy = pltpu.make_async_copy(src, dst, local_sem.at[i])
        copy.start()
        return copy

    def wait_for(ref, sem):
        pltpu.make_async_copy(ref, ref, sem).wait()

    own_cols = pl.ds(pl.multiple_of(core * H, H), H)
    other_cols = pl.ds(pl.multiple_of((1 - core) * H, H), H)

    def xi(arr, whose, h):
        return arr * 4 + whose * 2 + h

    for h in range(2):
        for arr, src in ((0, act_hbm), (1, og_hbm)):
            move(src.at[pl.ds(h * R, R)], x_buf.at[xi(arr, 0, h), par, x, yh], L_IN + h)
    weights = [
        move(wu_hbm.at[:, own_cols], wx.at[0], L_UP),
        move(wd_hbm.at[:, own_cols], wx.at[2], L_DOWN),
        move(wu_hbm.at[:, other_cols], wu_other, L_OTHER),
        move(bias_hbm, bias_buf, L_BIAS),
    ]

    barrier = pltpu.get_barrier_semaphore()
    peers = [sib, zp, zm] + [xpeer(k) for k in (1, 2, 3)] + [ypeer(k) for k in (1, 2, 3)]
    for peer in peers:
        pl.semaphore_signal(barrier, inc=1, device_id=peer, device_id_type=MESH)
    pl.semaphore_wait(barrier, len(peers))

    stage2 = {}

    def gather1(h):
        wait_for(x_buf.at[0, 0, 0], local_sem.at[L_IN + h])
        for k in (2, 1, 3):
            for arr, peer in ((0, xpeer(k)), (1, ypeer(k))):
                slot = x_buf.at[xi(arr, 0, h), par, x, yh]
                remote(slot, slot, peer, S_GATHER1, R_GATHER1 + h)

    def group(arr, whose, h, k):
        if arr == 0:
            yk = (y + 4 - k) % 4
            return x_buf.at[xi(0, whose, h), yk % 2, :, yk // 2]
        return x_buf.at[xi(1, whose, h), :, (x + 4 - k) % 4]

    def share(arr, h, k):
        remote(group(arr, 0, h, k), group(arr, 1, h, k), sib, S_SHARE, R_SHARE + h)

    def gather2(h):
        wait_for(x_buf.at[0, 0, pl.ds(0, 3)], recv_sem.at[R_GATHER1 + h])
        for k in (2, 1, 3):
            for arr, peer in ((0, ypeer(k)), (1, xpeer(k))):
                slot = group(arr, 0, h, 0)
                i = R_GATHER2 + (h * 2 + arr) * 3 + k - 1
                stage2[arr, h, k] = remote(slot, slot, peer, S_GATHER2, i)
        for arr in (0, 1):
            share(arr, h, 0)

    def gather3(h, *hops):
        for k in hops:
            for arr in (0, 1):
                stage2[arr, h, k].wait_recv()
                share(arr, h, k)

    def gathered(h):
        wait_for(x_buf.at[pl.ds(0, 2)], recv_sem.at[R_SHARE + h])

    def send_weights():
        remote(wu_hbm.at[:, other_cols], wx.at[1], sib, S_WEIGHTS, R_WEIGHTS)
        remote(wd_hbm.at[:, other_cols], wx.at[3], sib, S_WEIGHTS, R_WEIGHTS)

    def own_weights_ready():
        for copy in weights:
            copy.wait()

    def weights_ready():
        wait_for(wx.at[pl.ds(0, 2)], recv_sem.at[R_WEIGHTS])

    def project(h, whose):
        for ab in (0, 1):
            lhs = x_buf[xi(ab, whose, h)].reshape(256, H)

            total = jnp.dot(lhs, wx[ab * 2 + whose], preferred_element_type=F32)
            total = total.reshape(2, NZ, R, H)
            if whose == 1:
                total += part[h * 2 + ab]
            part[h * 2 + ab] = total

    up, down = {}, {}

    def chunk(q):
        return q // 4, q // 2 % 2, pl.ds(q % 2 * HALF, HALF)

    def chain_sem(q, way, step):
        return R_CHAIN + q * 4 + way * 2 + step % 2

    def reduce_step(q, s):
        h, p, c = chunk(q)
        if s > 0:
            up[q, s - 1].wait_recv()
            down[q, s - 1].wait_recv()
        for way, hops, send_buf, recv_buf, device in ((0, up, sp, rp, zp), (1, down, sm, rm, zm)):
            first = way
            owner = (z + 4 - s) % NZ if way == 0 else (z + 4 + s) % NZ
            for ab in (0, 1):
                if s == 0 and ab != first:
                    continue
                v = part[h * 2 + ab, p, owner, :, c]
                if s > 1 or (s == 1 and ab == first):
                    v = v + dec(recv_buf[q * 4 + s - 1, ab])
                send_buf[q * 4 + s, ab] = enc(v)
            which = pl.ds(first, 1) if s == 0 else pl.ds(0, 2)
            hops[q, s] = remote(
                send_buf.at[q * 4 + s, which], recv_buf.at[q * 4 + s, which], device,
                S_CHAIN, chain_sem(q, way, s),
            )

    fwd, bwd = {}, {}

    def to_sibling(q, owner):
        if q % 2 == 1:
            t = q // 2
            remote(
                g_buf.at[pl.ds(0, 2), t, owner], g_buf.at[pl.ds(2, 2), t, owner], sib,
                S_PAIR, R_PAIR + t,
            )

    def finish(q):
        h, p, c = chunk(q)
        up[q, 3].wait_recv()
        down[q, 3].wait_recv()
        both = [
            part[h * 2 + ab, p, z, :, c] + dec(rp[q * 4 + 3, ab]) + dec(rm[q * 4 + 3, ab])
            for ab in (0, 1)
        ]
        bias = bias_buf[...].astype(F32).reshape(1, 2 * H)
        bias = jnp.where(core == 0, bias[:, :H], bias[:, H:])[:, q % 2 * HALF : (q % 2 + 1) * HALF]
        value, slope = gelu_parts(both[0] + bias)
        g_buf[0, q // 2, z, :, c] = (both[1] * slope).astype(BF16)
        g_buf[1, q // 2, z, :, c] = value.astype(BF16)
        slot = g_buf.at[pl.ds(0, 2), q // 2, z, :, c]
        fwd[q, 0] = remote(slot, slot, zp, S_CHAIN, chain_sem(q, 0, 0))
        bwd[q, 0] = remote(slot, slot, zm, S_CHAIN, chain_sem(q, 1, 0))
        to_sibling(q, z)

    def spread_step(q, s):
        c = chunk(q)[2]
        fwd[q, s - 1].wait_recv()
        bwd[q, s - 1].wait_recv()
        owners = ((z + NZ - s) % NZ, (z + s) % NZ)
        for i, hops, device in ((0, fwd, zp), (1, bwd, zm)):
            which = pl.ds(i, 1) if s == 3 else pl.ds(0, 2)
            slot = g_buf.at[which, q // 2, owners[i], :, c]
            hops[q, s] = remote(slot, slot, device, S_CHAIN, chain_sem(q, i, s))
        for owner in owners:
            to_sibling(q, owner)

    def spread_last(q):
        fwd[q, 3].wait_recv()
        bwd[q, 3].wait_recv()
        to_sibling(q, (z + 4) % NZ)

    def spread_done(t):
        wait_for(g_buf.at[pl.ds(0, 2), t], recv_sem.at[R_PAIR + t])

    def backproject(h):
        grads = [g_buf[half * 2, pl.ds(2 * h, 2)].reshape(256, H) for half in (0, 1)]
        nt = (((1,), (1,)), ((), ()))

        total = lax.dot_general(grads[0], wx[0], nt, preferred_element_type=F32)
        total += lax.dot_general(grads[1], wu_other[...], nt, preferred_element_type=F32)
        ig_acc[h] = total.reshape(2, 4, 2, R, H)

    halves = (pl.ds(0, HALF), pl.ds(HALF, HALF))

    def rows_for(h, side, k):
        if side == 0:
            yk = (y + k) % 4
            return ig_acc[h, yk % 2, :, yk // 2, :, halves[0]]
        return ig_acc[h, :, (x + k) % 4, :, :, halves[1]].reshape(4, R, HALF)

    def scatter1(h):
        for k in (2, 1, 3):
            for side in (0, 1):
                i = (h * 2 + side) * 3 + k - 1
                s1[i] = enc(rows_for(h, side, k))
                remote(
                    s1.at[i], r1.at[i], (ypeer, xpeer)[side](k), S_NEAR, R_NEAR + h * 2 + side
                )

    def scatter2(h):
        for side in (0, 1):
            total = rows_for(h, side, 0)
            wait_for(r1.at[pl.ds(0, 3)], recv_sem.at[R_NEAR + h * 2 + side])
            for k in (1, 3, 2):
                total = total + dec(r1[(h * 2 + side) * 3 + k - 1])
            t1[side] = total
            for k in (2, 1, 3):
                i = (h * 2 + side) * 3 + k - 1
                if side == 0:
                    block = t1[0, (x + k) % 4]
                else:
                    yk = (y + k) % 4
                    block = t1[1, (yk % 2) * 2 + yk // 2]
                s2[i] = enc(block)
                remote(
                    s2.at[i], r2.at[i], (xpeer, ypeer)[side](k), S_FAR, R_FAR + h * 2 + side
                )

    def scatter3(h):
        for side in (0, 1):
            total = t1[0, x] if side == 0 else t1[1, par * 2 + yh]
            wait_for(r2.at[pl.ds(0, 3)], recv_sem.at[R_FAR + h * 2 + side])
            for k in (1, 3, 2):
                total = total + dec(r2[(h * 2 + side) * 3 + k - 1])
            ig_out[pl.ds(h * R, R), halves[side]] = total.astype(BF16)

    def weight_grad(arr, half):
        tokens = x_buf[pl.ds(xi(arr, 0, 0), 2)].reshape(512, H)
        grads = g_buf[half * 2 + arr].reshape(512, H)
        tn = (((0,), (0,)), ((), ()))
        total = lax.dot_general(tokens, grads, tn, preferred_element_type=F32)
        (up_out, down_out)[arr][half] = total.astype(BF16)

    def bias_grad():
        own, other = [
            jnp.sum(g_buf[i].reshape(512, H).astype(F32), axis=0, keepdims=True) for i in (0, 2)
        ]
        left, right = jnp.where(core == 0, own, other), jnp.where(core == 0, other, own)
        bias_out[...] = jnp.concatenate([left, right], axis=1).reshape(2 * H)

    def drain():
        for ref, i in (
            (x_buf.at[0, :, pl.ds(0, 3)], S_GATHER1),
            (x_buf.at[pl.ds(0, 3)], S_GATHER2),
            (x_buf.at[pl.ds(0, 4)], S_SHARE),
            (wx.at[pl.ds(0, 2)], S_WEIGHTS),
            (g_buf.at[:, :, pl.ds(0, 7)], S_CHAIN),
            (g_buf.at[pl.ds(0, 2)], S_PAIR),
            (s1, S_NEAR),
            (s2, S_FAR),
        ):
            wait_for(ref, send_sem.at[i])

    gather1(0)
    gather1(1)
    send_weights()
    gather2(0)
    gather3(0, 1)
    gather2(1)
    gather3(0, 3, 2)
    own_weights_ready()
    project(0, 0)
    weights_ready()
    gathered(0)
    project(0, 1)
    for q in range(4):
        reduce_step(q, 0)
    gather3(1, 1, 3, 2)
    for q in range(4):
        reduce_step(q, 1)
    project(1, 0)
    gathered(1)
    project(1, 1)
    for q in range(4):
        reduce_step(4 + q, 0)
    for q in range(4):
        reduce_step(q, 2)
    for q in range(4):
        reduce_step(4 + q, 1)
    for q in range(4):
        reduce_step(q, 3)
    for q in range(4):
        reduce_step(4 + q, 2)
    for q in range(4):
        finish(q)
    for q in range(4):
        reduce_step(4 + q, 3)
    for q in range(4):
        spread_step(q, 1)
    for q in range(4):
        finish(4 + q)
    for q in range(4):
        spread_step(q, 2)
    for q in range(4):
        spread_step(4 + q, 1)
    for q in range(4):
        spread_step(q, 3)
    for q in range(4):
        spread_step(4 + q, 2)
    for q in range(4):
        spread_last(q)
    for q in range(4):
        spread_step(4 + q, 3)
    spread_done(0)
    spread_done(1)
    backproject(0)
    scatter1(0)
    for q in range(4):
        spread_last(4 + q)
    scatter2(0)
    spread_done(2)
    spread_done(3)
    backproject(1)
    scatter1(1)
    scatter3(0)
    weight_grad(0, 0)
    weight_grad(0, 1)
    scatter2(1)
    weight_grad(1, 0)
    weight_grad(1, 1)
    bias_grad()
    scatter3(1)
    drain()


def place_kernel(up_ref, down_ref, bias_ref, ig_ref, up_hbm, down_hbm, bias_hbm, ig_hbm, sem):
    core = lax.axis_index("row") % 2
    copies = [
        pltpu.make_async_copy(bias_ref, bias_hbm, sem.at[4]),
        pltpu.make_async_copy(ig_ref, ig_hbm, sem.at[5]),
    ]
    for half in (0, 1):
        start = pl.multiple_of((core if half == 0 else 1 - core) * H, H)
        for arr, src, dst in ((0, up_ref, up_hbm), (1, down_ref, down_hbm)):
            cols = dst.at[:, pl.ds(start, H)]
            copies.append(pltpu.make_async_copy(src.at[half], cols, sem.at[half * 2 + arr]))
    for copy in copies:
        copy.start()
    for copy in copies:
        copy.wait()


def body(activations, output_grad, up_weight, down_weight, up_bias):
    anywhere = pl.BlockSpec(memory_space=pl.ANY)
    hbm = pl.BlockSpec(memory_space=pltpu.HBM)
    vmem = pl.BlockSpec(memory_space=pltpu.VMEM)
    operands = [
        pltpu.with_memory_space_constraint(a, pltpu.HBM)
        for a in (activations, output_grad, up_weight, down_weight, up_bias)
    ]
    results = pl.pallas_call(
        exchange_kernel,
        out_shape=[
            pltpu.VMEM((2, H, H), BF16),
            pltpu.VMEM((2, H, H), BF16),
            pltpu.VMEM((2 * H,), F32),
            pltpu.VMEM((2 * R, H), BF16),
        ],
        in_specs=[hbm] * 5,
        out_specs=[vmem] * 4,
        scratch_shapes=[
            pltpu.VMEM((8, 2, 4, 2, R, H), BF16),
            pltpu.VMEM((4, H, H), BF16),
            pltpu.VMEM((H, H), BF16),
            pltpu.VMEM((4, 2, NZ, R, H), F32),
            pltpu.VMEM((32, 2, R, HALF), BF16),
            pltpu.VMEM((32, 2, R, HALF), BF16),
            pltpu.VMEM((32, 2, R, HALF), BF16),
            pltpu.VMEM((32, 2, R, HALF), BF16),
            pltpu.VMEM((4, 4, NZ, R, H), BF16),
            pltpu.VMEM((2, 2, 4, 2, R, H), F32),
            pltpu.VMEM((12, 4, R, HALF), BF16),
            pltpu.VMEM((12, 4, R, HALF), BF16),
            pltpu.VMEM((2, 4, R, HALF), F32),
            pltpu.VMEM((12, R, HALF), BF16),
            pltpu.VMEM((12, R, HALF), BF16),
            pltpu.VMEM((2 * H,), BF16),
            pltpu.SemaphoreType.DMA((N_SEND,)),
            pltpu.SemaphoreType.DMA((N_RECV,)),
            pltpu.SemaphoreType.DMA((N_LOCAL,)),
        ],
        compiler_params=pltpu.CompilerParams(
            collective_id=0, has_side_effects=True, vmem_limit_bytes=44 << 20
        ),
        cost_estimate=pl.CostEstimate(
            flops=5 * 2 * 512 * H * 2 * H, bytes_accessed=12 << 20, transcendentals=64 * H
        ),
        name="exchange",
    )(*operands)
    up_grad, down_grad, bias_grad, input_grad = pl.pallas_call(
        place_kernel,
        out_shape=[
            jax.ShapeDtypeStruct((H, 2 * H), BF16),
            jax.ShapeDtypeStruct((H, 2 * H), BF16),
            jax.ShapeDtypeStruct((2 * H,), F32),
            jax.ShapeDtypeStruct((2 * R, H), BF16),
        ],
        in_specs=[anywhere] * 4,
        out_specs=[hbm] * 4,
        scratch_shapes=[pltpu.SemaphoreType.DMA((6,))],
        compiler_params=pltpu.CompilerParams(vmem_limit_bytes=1 << 20),
        cost_estimate=pl.CostEstimate(flops=0, bytes_accessed=5 << 20, transcendentals=0),
        name="place",
    )(*results)
    return (input_grad, up_grad, down_grad, bias_grad)


def solution(mesh):
    placed = (P("col", "row"), P("col", "row"), P("row", "col"), P("row", "col"), P("col"))
    return jax.shard_map(
        body,
        mesh=mesh,
        in_specs=placed,
        out_specs=(P("col", "row"), P("row", "col"), P("row", "col"), P("col")),
        check_vma=False,
    )
```

time: 85.2 us -> 72.3 us (0.85)
  Pallas kernels: 84.3 us -> 70.8 us
    pallas_call x2, Pallas kernels: 84.3 us -> 70.8 us  [the longest x1 68.5 us: body(): pl.pallas_call(exchange_kernel, out_shape=[pltpu.VMEM((2, H, H), BF16), p...]
where the time goes in v3:
time: 72.3 us; the launch traced here: 71.4 us
  Pallas kernels  70.8 us (98%)
    pallas_call x1, Pallas kernels, body(): pl.pallas_call(exchange_kernel, out_shape=[pltpu.VMEM((2, H, H), BF16), p...  68.5 us
    pallas_call x1, Pallas kernels, body(): pl.pallas_call(place_kernel, out_shape=[jax.ShapeDtypeStruct((H, 2 * H),...  2.25 us

profile of v3, /device:TPU:1, one launch (start us, length us, event | category | flops | bytes accessed | tf_op | source)
XLA Modules:
  0.0 71.4 jit_solution(13574524514870466440)
XLA Ops:
  0.6 68.5 %exchange.1 = (bf16[2,768,768]{2,1,0:T(8,128)(2,1)S(1)}, bf16[2,768,768]{2,1,0:T(8,128)(2,1)S(1)}, f32[1536]{0:T(1024)S(1)}, bf16[32,768]{1,0:T(8,128)(2,1)S(1)}) custom-call(bf16[32,768]{1,0:T(8,128)(2,1)} %act_hbm.1, bf16[32,768]{1,0:T(8,128)(2,1)} %og_hbm.1, bf16[768,1536]{1,0:T(8,128)(2,1)} %wu_hbm.1, bf16[768,1536]{1,0:T(8,128)(2,1)} %wd_hbm.1, ...), custom_call_target="tpu_custom_call" | custom-call | flops 6039797760 | bytes 12582912 | tf_op jit(solution)/shard_map/exchange/pallas_call | solution.py:418
  69.2 2.3 %place.1 = (bf16[768,1536]{1,0:T(8,128)(2,1)}, bf16[768,1536]{1,0:T(8,128)(2,1)}, f32[1536]{0:T(1024)}, bf16[32,768]{1,0:T(8,128)(2,1)}) custom-call(bf16[2,768,768]{2,1,0:T(8,128)(2,1)S(1)} %get-tuple-element.12.up_ref, bf16[2,768,768]{2,1,0:T(8,128)(2,1)S(1)} %get-tuple-element.13.down_ref, f32[1536]{0:T(1024)S(1)} %get-tuple-element.14.bias_ref, ...), custom_call_target="tpu_custom_call" | custom-call | bytes 5242880 | tf_op jit(solution)/shard_map/place/pallas_call | solution.py:457

commit v4 on v3

--- a/solution.py
+++ b/solution.py
@@ -270,14 +270,14 @@
             wait_for(r1.at[pl.ds(0, 3)], recv_sem.at[R_NEAR + h * 2 + side])
             for k in (1, 3, 2):
                 total = total + dec(r1[(h * 2 + side) * 3 + k - 1])
-            t1[side] = total
+            t1[h * 2 + side] = total
             for k in (2, 1, 3):
                 i = (h * 2 + side) * 3 + k - 1
                 if side == 0:
-                    block = t1[0, (x + k) % 4]
+                    block = t1[h * 2, (x + k) % 4]
                 else:
                     yk = (y + k) % 4
-                    block = t1[1, (yk % 2) * 2 + yk // 2]
+                    block = t1[h * 2 + 1, (yk % 2) * 2 + yk // 2]
                 s2[i] = enc(block)
                 remote(
                     s2.at[i], r2.at[i], (xpeer, ypeer)[side](k), S_FAR, R_FAR + h * 2 + side
@@ -285,7 +285,7 @@
 
     def scatter3(h):
         for side in (0, 1):
-            total = t1[0, x] if side == 0 else t1[1, par * 2 + yh]
+            total = t1[h * 2, x] if side == 0 else t1[h * 2 + 1, par * 2 + yh]
             wait_for(r2.at[pl.ds(0, 3)], recv_sem.at[R_FAR + h * 2 + side])
             for k in (1, 3, 2):
                 total = total + dec(r2[(h * 2 + side) * 3 + k - 1])
@@ -374,18 +374,18 @@
     scatter1(0)
     for q in range(4):
         spread_last(4 + q)
-    scatter2(0)
+    weight_grad(0, 0)
     spread_done(2)
     spread_done(3)
     backproject(1)
     scatter1(1)
-    scatter3(0)
-    weight_grad(0, 0)
+    scatter2(0)
     weight_grad(0, 1)
+    weight_grad(1, 0)
     scatter2(1)
-    weight_grad(1, 0)
     weight_grad(1, 1)
     bias_grad()
+    scatter3(0)
     scatter3(1)
     drain()
 
@@ -438,7 +438,7 @@
             pltpu.VMEM((2, 2, 4, 2, R, H), F32),
             pltpu.VMEM((12, 4, R, HALF), BF16),
             pltpu.VMEM((12, 4, R, HALF), BF16),
-            pltpu.VMEM((2, 4, R, HALF), F32),
+            pltpu.VMEM((4, 4, R, HALF), F32),
             pltpu.VMEM((12, R, HALF), BF16),
             pltpu.VMEM((12, R, HALF), BF16),
             pltpu.VMEM((2 * H,), BF16),

time: 72.3 us -> 72.2 us (level); the launches traced: 71.4 us -> 72.1 us
  no operation moved by 1% of the time
where the time goes in v4:
time: 72.2 us; the launch traced here: 72.1 us
  Pallas kernels  71.5 us (99%)
    pallas_call x1, Pallas kernels, body(): pl.pallas_call(exchange_kernel, out_shape=[pltpu.VMEM((2, H, H), BF16), p...  69.2 us
    pallas_call x1, Pallas kernels, body(): pl.pallas_call(place_kernel, out_shape=[jax.ShapeDtypeStruct((H, 2 * H),...  2.25 us

profile of v4, /device:TPU:1, one launch (start us, length us, event | category | flops | bytes accessed | tf_op | source)
XLA Modules:
  0.0 72.1 jit_solution(2407896420832203442)
XLA Ops:
  0.6 69.2 %exchange.1 = (bf16[2,768,768]{2,1,0:T(8,128)(2,1)S(1)}, bf16[2,768,768]{2,1,0:T(8,128)(2,1)S(1)}, f32[1536]{0:T(1024)S(1)}, bf16[32,768]{1,0:T(8,128)(2,1)S(1)}) custom-call(bf16[32,768]{1,0:T(8,128)(2,1)} %act_hbm.1, bf16[32,768]{1,0:T(8,128)(2,1)} %og_hbm.1, bf16[768,1536]{1,0:T(8,128)(2,1)} %wu_hbm.1, bf16[768,1536]{1,0:T(8,128)(2,1)} %wd_hbm.1, ...), custom_call_target="tpu_custom_call" | custom-call | flops 6039797760 | bytes 12582912 | tf_op jit(solution)/shard_map/exchange/pallas_call | solution.py:418
  69.9 2.3 %place.1 = (bf16[768,1536]{1,0:T(8,128)(2,1)}, bf16[768,1536]{1,0:T(8,128)(2,1)}, f32[1536]{0:T(1024)}, bf16[32,768]{1,0:T(8,128)(2,1)}) custom-call(bf16[2,768,768]{2,1,0:T(8,128)(2,1)S(1)} %get-tuple-element.12.up_ref, bf16[2,768,768]{2,1,0:T(8,128)(2,1)S(1)} %get-tuple-element.13.down_ref, f32[1536]{0:T(1024)S(1)} %get-tuple-element.14.bias_ref, ...), custom_call_target="tpu_custom_call" | custom-call | bytes 5242880 | tf_op jit(solution)/shard_map/place/pallas_call | solution.py:457

commit v5 on v4

--- a/solution.py
+++ b/solution.py
@@ -239,13 +239,15 @@
     def spread_done(t):
         wait_for(g_buf.at[pl.ds(0, 2), t], recv_sem.at[R_PAIR + t])
 
-    def backproject(h):
-        grads = [g_buf[half * 2, pl.ds(2 * h, 2)].reshape(256, H) for half in (0, 1)]
+    def backproject(h, half):
+        grads = g_buf[half * 2, pl.ds(2 * h, 2)].reshape(256, H)
+        weight = (wx.at[0], wu_other)[half][...]
         nt = (((1,), (1,)), ((), ()))
-
-        total = lax.dot_general(grads[0], wx[0], nt, preferred_element_type=F32)
-        total += lax.dot_general(grads[1], wu_other[...], nt, preferred_element_type=F32)
-        ig_acc[h] = total.reshape(2, 4, 2, R, H)
+        total = lax.dot_general(grads, weight, nt, preferred_element_type=F32)
+        total = total.reshape(2, 4, 2, R, H)
+        if half == 1:
+            total += ig_acc[h]
+        ig_acc[h] = total
 
     halves = (pl.ds(0, HALF), pl.ds(HALF, HALF))
 
@@ -370,14 +372,16 @@
         spread_step(4 + q, 3)
     spread_done(0)
     spread_done(1)
-    backproject(0)
+    backproject(0, 0)
+    backproject(0, 1)
     scatter1(0)
     for q in range(4):
         spread_last(4 + q)
+    backproject(1, 0)
     weight_grad(0, 0)
     spread_done(2)
     spread_done(3)
-    backproject(1)
+    backproject(1, 1)
     scatter1(1)
     scatter2(0)
     weight_grad(0, 1)

time: 72.2 us -> 71.6 us (level)
  no operation moved by 1% of the time
where the time goes in v5:
time: 71.6 us; the launch traced here: 71.5 us
  Pallas kernels  70.9 us (99%)
    pallas_call x1, Pallas kernels, body(): pl.pallas_call(exchange_kernel, out_shape=[pltpu.VMEM((2, H, H), BF16), p...  68.6 us
    pallas_call x1, Pallas kernels, body(): pl.pallas_call(place_kernel, out_shape=[jax.ShapeDtypeStruct((H, 2 * H),...  2.25 us

profile of v5, /device:TPU:1, one launch (start us, length us, event | category | flops | bytes accessed | tf_op | source)
XLA Modules:
  0.0 71.5 jit_solution(15458020290718569569)
XLA Ops:
  0.6 68.6 %exchange.1 = (bf16[2,768,768]{2,1,0:T(8,128)(2,1)S(1)}, bf16[2,768,768]{2,1,0:T(8,128)(2,1)S(1)}, f32[1536]{0:T(1024)S(1)}, bf16[32,768]{1,0:T(8,128)(2,1)S(1)}) custom-call(bf16[32,768]{1,0:T(8,128)(2,1)} %act_hbm.1, bf16[32,768]{1,0:T(8,128)(2,1)} %og_hbm.1, bf16[768,1536]{1,0:T(8,128)(2,1)} %wu_hbm.1, bf16[768,1536]{1,0:T(8,128)(2,1)} %wd_hbm.1, ...), custom_call_target="tpu_custom_call" | custom-call | flops 6039797760 | bytes 12582912 | tf_op jit(solution)/shard_map/exchange/pallas_call | solution.py:422
  69.2 2.3 %place.1 = (bf16[768,1536]{1,0:T(8,128)(2,1)}, bf16[768,1536]{1,0:T(8,128)(2,1)}, f32[1536]{0:T(1024)}, bf16[32,768]{1,0:T(8,128)(2,1)}) custom-call(bf16[2,768,768]{2,1,0:T(8,128)(2,1)S(1)} %get-tuple-element.12.up_ref, bf16[2,768,768]{2,1,0:T(8,128)(2,1)S(1)} %get-tuple-element.13.down_ref, f32[1536]{0:T(1024)S(1)} %get-tuple-element.14.bias_ref, ...), custom_call_target="tpu_custom_call" | custom-call | bytes 5242880 | tf_op jit(solution)/shard_map/place/pallas_call | solution.py:461
